TPU v7x, 512 devices: a whole 4x4x16 slice. The times are simulated.
512 devices in a mesh: beam: 32 (over x, z_lo), tile: 16 (over z_hi, y, core).
Axes of the slice: x: 4, y: 4, z: 16 (z_hi: 2, z_lo: 8; z = z_hi * 8 + z_lo), core: 2. Of those that a mesh axis runs over, the one named last changes fastest.
Arguments:
- atom_counts: bfloat16 [2, 512, 4096], P(None, 'tile'), may hold values from 0 to 4
- beam_index: int32 [32, 2], P('beam'), may hold values from -16 to 16
- beam_weight: float32 [32], P('beam'), may hold values from 0.3 to 3
- probe_rows: int32 [1024], P('tile'), may hold values from 0 to 16
- probe_cols: int32 [1024], P('tile'), may hold values from 0 to 4095
Outputs:
- intensity: float32 [1024, 256], P('tile', 'beam')
All inputs are finite; a program needn't handle non-finite values.
Results may differ from a plain program's by a relative error of at most 0.0003.
Values may be sent and summed in bfloat16 or wider, within the bound.
A program may use at most 64 MiB of HBM per device.

v0:
```python
import math

import jax
import jax.numpy as jnp
from jax import lax
from jax.sharding import PartitionSpec as P

CROP = 16


def extended(block, sides, width):
    for axis, dim in sides:
        count = lax.axis_size(axis)
        forward = [(i, i + 1) for i in range(count - 1)]
        forward.append((count - 1, 0))
        backward = [(target, source) for source, target in forward]
        low = lax.ppermute(
            lax.slice_in_dim(block, block.shape[dim] - width, None, axis=dim), axis, forward
        )
        high = lax.ppermute(lax.slice_in_dim(block, 0, width, axis=dim), axis, backward)
        block = jnp.concatenate([low, block, high], axis=dim)
    return block


def cut_along(x, dim, peers):
    shape = x.shape
    parts = x.reshape(*shape[:dim], peers, shape[dim] // peers, *shape[dim + 1 :])
    return jnp.moveaxis(parts, dim, 0)


def summed_on_arrival(x, axis, dim):
    peers = lax.axis_size(axis)
    parts = lax.all_to_all(cut_along(x, dim, peers), axis, 0, 0, tiled=True)
    return jnp.sum(parts, axis=0)


def make_taps():
    blur_raw = [math.exp(-((offset_index - 5) ** 2) / 4.5) for offset_index in range(11)]
    blur_total = sum(blur_raw)
    spread_raw = [math.exp(-((offset_index - 5) ** 2) / 18.0) for offset_index in range(11)]
    spread_total = sum(spread_raw)
    blur_list = [entry_value / blur_total for entry_value in blur_raw]
    cos_list = [
        spread_raw[offset_index] / spread_total * math.cos(0.35 * (offset_index - 5) ** 2)
        for offset_index in range(11)
    ]
    sin_list = [
        spread_raw[offset_index] / spread_total * math.sin(0.35 * (offset_index - 5) ** 2)
        for offset_index in range(11)
    ]
    return (blur_list, cos_list, sin_list)


def spread_columns(real_part, imag_part):
    blur_taps, cos_taps, sin_taps = make_taps()
    out_real = jnp.zeros_like(real_part)
    out_imag = jnp.zeros_like(imag_part)
    for offset_index in range(11):
        shift_real = jnp.roll(real_part, 5 - offset_index, axis=-1)
        shift_imag = jnp.roll(imag_part, 5 - offset_index, axis=-1)
        out_real = (
            out_real + cos_taps[offset_index] * shift_real - sin_taps[offset_index] * shift_imag
        )
        out_imag = (
            out_imag + cos_taps[offset_index] * shift_imag + sin_taps[offset_index] * shift_real
        )
    return (out_real, out_imag)


def spread_rows(padded_real, padded_imag):
    blur_taps, cos_taps, sin_taps = make_taps()
    out_rows = padded_real.shape[1] - 10
    out_real = jnp.zeros_like(padded_real[:, 0:out_rows])
    out_imag = jnp.zeros_like(padded_imag[:, 0:out_rows])
    for offset_index in range(11):
        shift_real = padded_real[:, offset_index : offset_index + out_rows]
        shift_imag = padded_imag[:, offset_index : offset_index + out_rows]
        out_real = (
            out_real + cos_taps[offset_index] * shift_real - sin_taps[offset_index] * shift_imag
        )
        out_imag = (
            out_imag + cos_taps[offset_index] * shift_imag + sin_taps[offset_index] * shift_real
        )
    return (out_real, out_imag)


def body(atom_counts, beam_index, beam_weight, probe_rows, probe_cols):
    blur_taps, cos_taps, sin_taps = make_taps()
    slice_count = atom_counts.shape[0]
    strip_rows = atom_counts.shape[1]
    grid_cols = atom_counts.shape[2]
    grid_rows = strip_rows * lax.axis_size("tile")
    first_row = lax.axis_index("tile") * strip_rows
    beam_total = beam_weight.shape[0] * lax.axis_size("beam")
    margin = 5 * slice_count
    padded_counts = extended(atom_counts, (("tile", 1),), margin + 5)
    extent_rows = strip_rows + 2 * margin
    counts_float = padded_counts.astype(jnp.float32)
    along_rows = blur_taps[0] * counts_float[:, 0:extent_rows]
    for offset_index in range(1, 11):
        along_rows = (
            along_rows
            + blur_taps[offset_index] * counts_float[:, offset_index : offset_index + extent_rows]
        )
    blurred = blur_taps[0] * jnp.roll(along_rows, 5, axis=-1)
    for offset_index in range(1, 11):
        blurred = blurred + blur_taps[offset_index] * jnp.roll(
            along_rows, 5 - offset_index, axis=-1
        )
    local_rows = (first_row - margin + jnp.arange(extent_rows, dtype=jnp.int32)) % grid_rows
    col_grid = jnp.arange(grid_cols, dtype=jnp.int32)
    row_phase = (beam_index[:, 0:1] * local_rows[None, :] % grid_rows).astype(
        jnp.float32
    ) / grid_rows
    col_phase = (beam_index[:, 1:2] * col_grid[None, :] % grid_cols).astype(jnp.float32) / grid_cols
    angle_grid = 2.0 * math.pi * (row_phase[:, :, None] + col_phase[:, None, :])
    real_part = jnp.cos(angle_grid)
    imag_part = jnp.sin(angle_grid)
    for slice_index in range(slice_count):
        reach_rows = margin - 5 * slice_index
        start_row = margin - reach_rows
        length_rows = strip_rows + 2 * reach_rows
        phase_now = 0.6 * blurred[slice_index, start_row : start_row + length_rows]
        cos_now = jnp.cos(phase_now)
        sin_now = jnp.sin(phase_now)
        real_part, imag_part = (
            real_part * cos_now - imag_part * sin_now,
            real_part * sin_now + imag_part * cos_now,
        )
        padded_real, padded_imag = (real_part, imag_part)
        real_part, imag_part = spread_rows(padded_real, padded_imag)
        real_part, imag_part = spread_columns(real_part, imag_part)
    probe_count = probe_rows.shape[0]
    crop_rows = probe_rows[:, None] + jnp.arange(CROP, dtype=jnp.int32)[None, :]
    crop_cols = (probe_cols[:, None] + jnp.arange(CROP, dtype=jnp.int32)[None, :]) % grid_cols
    crop_real = real_part[:, crop_rows[:, :, None], crop_cols[:, None, :]]
    crop_imag = imag_part[:, crop_rows[:, :, None], crop_cols[:, None, :]]
    global_rows = first_row + probe_rows
    probe_phase = (
        2.0
        * math.pi
        * (
            (beam_index[:, 0:1] * global_rows[None, :] % grid_rows).astype(jnp.float32) / grid_rows
            + (beam_index[:, 1:2] * probe_cols[None, :] % grid_cols).astype(jnp.float32) / grid_cols
        )
    )
    coef_real = beam_weight[:, None] * jnp.cos(probe_phase)
    coef_imag = -beam_weight[:, None] * jnp.sin(probe_phase)
    exit_real = jnp.einsum("bp,bpuv->puv", coef_real, crop_real) - jnp.einsum(
        "bp,bpuv->puv", coef_imag, crop_imag
    )
    exit_imag = jnp.einsum("bp,bpuv->puv", coef_real, crop_imag) + jnp.einsum(
        "bp,bpuv->puv", coef_imag, crop_real
    )
    terms = jnp.stack([exit_real, exit_imag], axis=1).reshape(probe_count, 2, CROP * CROP)
    summed = summed_on_arrival(terms, "beam", 2)
    return (summed[:, 0] * summed[:, 0] + summed[:, 1] * summed[:, 1]) / beam_total


def solution(mesh):
    return jax.shard_map(
        body,
        mesh=mesh,
        in_specs=(P(None, "tile", None), P("beam", None), P("beam"), P("tile"), P("tile")),
        out_specs=P("tile", "beam"),
        check_vma=False,
    )
```

profile of v0, /device:TPU:25, one launch (start us, length us, event | category | flops | bytes accessed | tf_op | source)
XLA Modules:
  0.0 384.5 jit_solution(12465904815508249410)
XLA Ops:
  0.0 1.1 fusion.107
  1.2 15.7 %collective-permute-start = (bf16[2,15,4096]{2,1,0:T(8,128)(2,1)S(1)}, bf16[2,15,4096]{2,1,0:T(8,128)(2,1)S(1)}, u32[]{:S(2)}, u32[]{:S(2)}) collective-permute-start(bf16[2,15,4096]{2,1,0:T(8,128)(2,1)S(1)} %get-tuple-element.112), channel_id=1, source_target_pairs={{0,1},{1,2},{2,3},{3,4},{4,5},{5,6},{6,7},{7,8},{8,9},{9,10},{10,1... | collective-permute-start | bytes 737288 | tf_op jit(solution)/shard_map/ppermute | solution.py:17
  16.8 1.9 collective-permute-start.1
  18.8 1.3 fusion.108
  20.0 0.6 fusion.36
  21.3 0.8 fusion.28
  22.3 2.5 cosine_multiply_fusion
  24.7 0.7 fusion.50
  25.6 0.6 sine_multiply_fusion
  26.2 11.2 %collective-permute-done.1 = bf16[2,15,4096]{2,1,0:T(8,128)(2,1)S(1)} collective-permute-done((bf16[2,15,4096]{2,1,0:T(8,128)(2,1)S(1)}, bf16[2,15,4096]{2,1,0:T(8,128)(2,1)S(1)}, u32[]{:S(2)}, u32[]{:S(2)}) %collective-permute-start.1) | collective-permute-done | bytes 245792 | tf_op jit(solution)/shard_map/ppermute | solution.py:20
  37.7 2.4 fusion
  40.1 0.6 fusion.57
  40.7 0.6 fusion.59
  41.3 2.4 fusion.61
  43.8 2.4 fusion.63
  46.2 2.5 fusion.65
  49.1 10.5 %fusion.19 = f32[2,52,4096]{2,1,0:T(8,128)S(1)} fusion(f32[2,52,4091]{2,1,0:T(8,128)S(1)} %get-tuple-element.13, f32[2,52,5]{2,1,0:T(8,128)S(1)} %get-tuple-element.15, f32[2,52,4092]{2,1,0:T(8,128)S(1)} %get-tuple-element.17, f32[2,52,4]{2,1,0:T(8,128)S(1)} %get-tuple-element.19, f32[2,52,4093]{2,1,0:T(8,128)} %get-tuple-element.21, ...), kind=kLoop, calls=%fused_computation.33 | loop fusion | flops 22151168 | bytes 37486592 | tf_op jit(solution)/shard_map/add | solution.py:107
  59.6 6.6 %multiply_subtract_fusion = (f32[1,52,4096]{2,1,0:T(8,128)S(1)}, f32[1,52,4096]{2,1,0:T(8,128)S(1)}) fusion(f32[2,52,4096]{2,1,0:T(8,128)S(1)} %fusion.19, f32[4096]{0:T(1024)S(1)} %fusion.36, f32[52]{0:T(128)S(1)} %fusion.50), kind=kLoop, calls=%fused_computation.46 | loop fusion | flops 1916928 | bytes 2572496 | tf_op jit(solution)/shard_map/sub | solution.py:127
  66.1 2.1 multiply_add_fusion.3
  68.2 2.1 multiply_subtract_fusion.3
  73.3 9.7 %multiply_subtract_fusion.1 = (f32[1,42,4096]{2,1,0:T(8,128)S(1)}, f32[1,42,4096]{2,1,0:T(8,128)S(1)}, f32[1,42,4096]{2,1,0:T(8,128)S(1)}) fusion(f32[2,52,4096]{2,1,0:T(8,128)S(1)} %fusion.19, f32[1,42,5]{2,1,0:T(8,128)S(1)} %get-tuple-element.118, f32[1,42,4091]{2,1,0:T(8,128)S(1)} %get-tuple-element.120, f32[1,42,5]{2,1,0:T(8,128)S(1)} %get-tuple-element.33, ...), kind=kLoop, calls=%fused_computation.74 | loop fusion | flops 18923520 | bytes 17891328 | tf_op jit(solution)/shard_map/sub | solution.py:127
  83.1 3.0 multiply_add_fusion.1
  86.1 1.2 multiply_add_fusion.4
  88.3 1.2 multiply_subtract_fusion.4
  91.3 2.3 subtract_bitcast_fusion
  93.6 3.0 add_bitcast_fusion
  96.6 129.5 %gather_fusion = f32[16384]{0:T(1024)S(1)} fusion(f32[32,4096]{1,0:T(8,128)S(1)} %subtract_bitcast_fusion, s32[16384]{0:T(1024)S(1)} %reshape.2673), kind=kCustom, calls=%fused_computation | custom fusion | bytes 262144 | tf_op jit(solution)/shard_map/gather | solution.py:136
  226.2 0.9 copy.11
  227.1 129.5 %gather_fusion.1 = f32[16384]{0:T(1024)S(1)} fusion(f32[32,4096]{1,0:T(8,128)S(1)} %copy-done, s32[16384]{0:T(1024)S(1)} %reshape.2673), kind=kCustom, calls=%fused_computation.1 | custom fusion | bytes 262144 | tf_op jit(solution)/shard_map/gather | solution.py:137
  357.3 25.0 %all_to_all.5 = f32[32,1,1024]{2,1,0:T(1,128)S(1)} all-to-all(f32[32,1,1024]{2,1,0:T(1,128)S(1)} %reshape.2691), channel_id=1, replica_groups=mesh['beam'=32,'tile'=16] {'beam'}, dimensions={0} | all-to-all | bytes 262144 | tf_op jit(solution)/shard_map/all_to_all | solution.py:33
  382.8 0.9 reduce
  383.9 0.6 fusion.42
  (58 shorter events, 8.4 us)
Async XLA Ops:
  0.0 37.4 %copy-start.1 = (bf16[2,32,4096]{2,1,0:T(8,128)(2,1)S(1)}, bf16[2,32,4096]{2,1,0:T(8,128)(2,1)}, u32[]{:S(2)}) copy-start(bf16[2,32,4096]{2,1,0:T(8,128)(2,1)} %param.5) | copy-start | bytes 1572868
  1.2 25.0 %collective-permute-start = (bf16[2,15,4096]{2,1,0:T(8,128)(2,1)S(1)}, bf16[2,15,4096]{2,1,0:T(8,128)(2,1)S(1)}, u32[]{:S(2)}, u32[]{:S(2)}) collective-permute-start(bf16[2,15,4096]{2,1,0:T(8,128)(2,1)S(1)} %get-tuple-element.112), channel_id=1, source_target_pairs={{0,1},{1,2},{2,3},{3,4},{4,5},{5,6},{6,7},{7,8},{8,9},{9,10},{10,1... | collective-permute-start | bytes 737288 | tf_op jit(solution)/shard_map/ppermute | solution.py:17
  16.8 20.6 %collective-permute-start.1 = (bf16[2,15,4096]{2,1,0:T(8,128)(2,1)S(1)}, bf16[2,15,4096]{2,1,0:T(8,128)(2,1)S(1)}, u32[]{:S(2)}, u32[]{:S(2)}) collective-permute-start(bf16[2,15,4096]{2,1,0:T(8,128)(2,1)S(1)} %get-tuple-element.113), channel_id=1, source_target_pairs={{1,0},{2,1},{3,2},{4,3},{5,4},{6,5},{7,6},{8,7},{9,8},{10,9},{11,1... | collective-permute-start | bytes 737288 | tf_op jit(solution)/shard_map/ppermute | solution.py:20
  226.0 1.1 copy-start
  227.1 129.9 %copy-start.2 = (f32[64,16,16]{0,2,1:T(8,128)S(1)}, f32[64,16,16]{0,2,1:T(8,128)}, u32[]{:S(2)}) copy-start(f32[64,16,16]{0,2,1:T(8,128)} %copy.11) | copy-start | bytes 196612
  227.1 129.9 %copy-start.3 = (f32[64]{0:T(128)S(1)}, f32[64]{0:T(128)}, u32[]{:S(2)}) copy-start(f32[64]{0:T(128)} %get-tuple-element.5) | copy-start | bytes 772
  227.1 129.9 %copy-start.4 = (f32[64]{0:T(128)S(1)}, f32[64]{0:T(128)}, u32[]{:S(2)}) copy-start(f32[64]{0:T(128)} %sine_multiply_fusion) | copy-start | bytes 772
where the time goes:
time: 385 us
  local copies, waits for them, and re-layouts  279 us (72%)
  other arithmetic  51.1 us (13%)
  blocking collectives  25 us (6%)
  starting transfers between devices  17.6 us (5%)
  waiting for transfers between devices  11.2 us (3%)
    gather x1, local copies, waits for them, and re-layouts, body(): crop_imag = imag_part[:, crop_rows[:, :, None], crop_cols[:, None, :]]  129 us
    gather x1, local copies, waits for them, and re-layouts, body(): crop_real = real_part[:, crop_rows[:, :, None], crop_cols[:, None, :]]  129 us
    all_to_all x1, blocking collectives, summed_on_arrival(): parts = lax.all_to_all(cut_along(x, dim, peers), axis, 0, 0, tiled=True)  25 us
    sub x2, other arithmetic, body(): real_part * cos_now - imag_part * sin_now  16.3 us
    ppermute x1, starting transfers between devices, extended(): lax.ppermute(lax.slice_in_dim(block, block.shape[dim] - width, None, axis...  15.7 us
    ppermute x1, waiting for transfers between devices, extended(): lax.ppermute(lax.slice_in_dim(block, 0, width, axis=dim), axis, backward)  11.2 us
    add x1, other arithmetic, body(): blurred + blur_taps[offset_index] * jnp.roll(along_rows, 5 - offset_index...  10.5 us
    slice x10, local copies, waits for them, and re-layouts, body(): jnp.roll(along_rows, 5 - offset_index, axis=-1)  9.03 us
  transfers between devices with their start and end apart: 2, of which 1 were waited for; matrix products, arithmetic and copies ran while one was open for 2% of the time, Pallas kernels for 0%

commit v1 on v0

v1 whole, which is shorter than its diff:
```python
import functools
import math

import jax
import jax.numpy as jnp
import numpy as np
from jax import lax
from jax.experimental import pallas as pl
from jax.experimental.pallas import tpu as pltpu
from jax.sharding import PartitionSpec as P

CROP = 16
REACH = 5
HALO = 16
CENTRE = 1.2
F32 = jnp.float32
BF16 = jnp.bfloat16


def make_taps():
    offsets = np.arange(-REACH, REACH + 1, dtype=np.float64)
    blur = np.exp(-(offsets**2) / 4.5)
    blur = blur / blur.sum()
    weight = np.exp(-(offsets**2) / 18.0)
    weight = weight / weight.sum()
    spread = weight * np.exp(1j * 0.35 * offsets**2)
    return blur, spread


def fit(function, limit, terms):
    nodes = 0.5 * limit * (1.0 + np.cos(np.pi * (np.arange(64) + 0.5) / 64))
    return np.polynomial.Polynomial.fit(nodes, function(nodes), terms - 1, domain=[0, limit]).convert().coef


def horner(coefs, x):
    result = jnp.full_like(x, float(coefs[-1]))
    for coef in coefs[-2::-1]:
        result = result * x + float(coef)
    return result


def cos_sin_small(t):
    square = t * t
    root = np.sqrt
    even = fit(lambda s: np.cos(root(s)), 1.69, 6)
    odd = fit(lambda s: np.sin(root(s)) / root(s), 1.69, 5)
    return horner(even, square), t * horner(odd, square)


def cos_sin_turns(turns):
    turns = turns - jnp.floor(turns + 0.5)
    square = turns * turns
    full = lambda s: 2.0 * np.pi * np.sqrt(s)
    even = fit(lambda s: np.cos(full(s)), 0.25, 9)
    odd = fit(lambda s: np.sin(full(s)) / np.sqrt(s), 0.25, 8)
    return horner(even, square), turns * horner(odd, square)


def band(distance, values):
    result = jnp.zeros(distance.shape, F32)
    reach = jnp.abs(distance)
    for k in range(REACH + 1):
        result = jnp.where(reach == k, float(values[REACH + k]), result)
    return result


def split(x):
    high = x.astype(BF16)
    return high, (x - high.astype(F32)).astype(BF16)


def blur_matrix(shift):
    blur, _ = make_taps()
    rows = lax.broadcasted_iota(jnp.int32, (128, 128), 0)
    cols = lax.broadcasted_iota(jnp.int32, (128, 128), 1)
    values = band(rows - cols - shift - REACH, 0.6 * blur)
    high, low = split(jnp.where(rows // 64 == cols // 64, values, 0.0))
    return jnp.concatenate([high, low], axis=1)


def spread_matrix():
    _, spread = make_taps()
    turned = spread * np.exp(1j * CENTRE)
    rows = lax.broadcasted_iota(jnp.int32, (128, 128), 0)
    cols = lax.broadcasted_iota(jnp.int32, (128, 128), 1)
    same = rows // 64 == cols // 64
    distance = rows - cols - REACH
    real = jnp.where(same, band(distance, turned.real), 0.0)
    imag = jnp.where(same, band(distance, turned.imag), 0.0)
    whole = jnp.concatenate(
        [jnp.concatenate([real, imag], axis=1), jnp.concatenate([-imag, real], axis=1)], axis=0
    )
    return split(whole)


def dot(a, b):
    return jnp.dot(a, b, preferred_element_type=F32)


def dot3(x, high, low):
    x_high, x_low = split(x)
    return dot(x_high, high) + dot(x_low, high) + dot(x_high, low)


def blur_rows(x):
    blur, _ = make_taps()
    rows = x.shape[0] - 2 * REACH
    result = float(blur[REACH]) * x[REACH : REACH + rows]
    for k in range(REACH):
        far = 2 * REACH - k
        result = result + float(blur[k]) * (x[k : k + rows] + x[far : far + rows])
    return result


def spread_rows(real, imag):
    _, spread = make_taps()
    rows = real.shape[0] - 2 * REACH
    out_real, out_imag = 0.0, 0.0
    for k in range(REACH + 1):
        near, far = k, 2 * REACH - k
        a, b = real[near : near + rows], imag[near : near + rows]
        if near != far:
            a, b = a + real[far : far + rows], b + imag[far : far + rows]
        c, s = float(spread[k].real), float(spread[k].imag)
        out_real = out_real + (c * a - s * b)
        out_imag = out_imag + (c * b + s * a)
    return out_real, out_imag


def place_rows(ext, source, first, extent):
    slices, rows, cols = source.shape
    tiles = cols // 128

    def one(tile, carry):
        for s in range(slices):
            block = source[s, :, pl.ds(pl.multiple_of(tile * 128, 128), 128)]
            start = pl.multiple_of((s * tiles + tile) * extent + first, 16)
            ext[pl.ds(start, rows), :] = block.astype(F32)
        return carry

    lax.fori_loop(0, tiles, one, 0, unroll=4)


def take_windows(ext, extent, tiles, probe_rows, probe_cols, gathered, slice_index, first, row_count, u, half):
    cols_total = tiles * 128
    pairs = probe_rows.shape[0] // 2
    lane = lax.broadcasted_iota(jnp.int32, (row_count, 128), 1)

    def window(probe, place):
        start = lax.rem(probe_cols[probe] + 8 * half - 3 * REACH + cols_total, cols_total)
        tile, offset = start // 128, lax.rem(start, 128)
        after = lax.rem(tile + 1, tiles)
        row = probe_rows[probe] + u + first
        near = ext[pl.ds((slice_index * tiles + tile) * extent + row, row_count), :]
        far = ext[pl.ds((slice_index * tiles + after) * extent + row, row_count), :]
        both = jnp.where(lane >= offset, near, far)
        return pltpu.roll(both, lax.rem(128 - offset + place, 128), 1)

    def one(pair, carry):
        joined = jnp.where(lane < 64, window(pair, 0), window(pair + pairs, 64))
        gathered[pl.ds(pair, row_count, stride=pairs), :] = joined
        return carry

    lax.fori_loop(0, pairs, one, 0, unroll=4)


def transmission(gathered, shift):
    pairs = 32
    blurred = dot(gathered[...].astype(BF16), blur_matrix(shift))
    blurred = blurred[:, :128] + blurred[:, 128:]
    rows = blurred.reshape(gathered.shape[0] // pairs, pairs, 128)
    rows = rows[: rows.shape[0] - (1 if shift == 0 else 3)]
    return cos_sin_small(blur_rows(rows) - CENTRE)


def probe_function(table, u, half):
    kx, ky, weight = table[:, 0:1], table[:, 1:2], table[:, 2:3]
    lane = lax.broadcasted_iota(jnp.int32, (table.shape[0], 128), 1)
    down = (lane + (u - 2 * REACH)).astype(F32)
    across = (lax.rem(lane, 64) + (8 * half - 2 * REACH)).astype(F32)
    row_cos, row_sin = cos_sin_turns(kx * down * (1.0 / 512.0))
    col_cos, col_sin = cos_sin_turns(ky * across * (1.0 / 4096.0))
    left = jnp.concatenate([weight * row_cos, weight * row_sin], axis=0)
    right = jnp.concatenate(
        [
            jnp.concatenate([col_cos, col_sin], axis=1),
            jnp.concatenate([-col_sin, col_cos], axis=1),
        ],
        axis=0,
    )
    return lax.dot_general(
        left, right, (((0,), (0,)), ((), ())), precision=lax.Precision.HIGHEST,
        preferred_element_type=F32,
    )


def propagate(wave, first_cos, first_sin, second_cos, second_sin, beams):
    pairs = first_cos.shape[1]
    high, low = spread_matrix()
    rows = first_cos.shape[0]
    wave_real = wave[:rows, None, :128]
    wave_imag = wave[:rows, None, 128:]
    real = first_cos * wave_real - first_sin * wave_imag
    imag = first_cos * wave_imag + first_sin * wave_real
    real, imag = spread_rows(real, imag)
    rows = real.shape[0]
    both = jnp.concatenate([real, imag], axis=2).reshape(rows * pairs, 256)
    both = dot3(both, high, low).reshape(rows, pairs, 256)
    real, imag = both[:, :, :128], both[:, :, 128:]
    real, imag = real * second_cos - imag * second_sin, real * second_sin + imag * second_cos
    real, imag = spread_rows(real, imag)
    both = dot3(jnp.concatenate([real[0], imag[0]], axis=1), high, low)
    return (both[:, :128] * both[:, :128] + both[:, 128:] * both[:, 128:]) * (1.0 / beams)


def kernel(probe_rows, probe_cols, own, prev, following, table, out, ext, first, second):
    beam = lax.axis_index("beam")
    u, half = beam // 2, lax.rem(beam, 2)
    strip = own.shape[1]
    tiles = own.shape[2] // 128
    extent = strip + 2 * HALO
    place_rows(ext, prev, 0, extent)
    place_rows(ext, own, HALO, extent)
    place_rows(ext, following, HALO + strip, extent)
    take_windows(ext, extent, tiles, probe_rows, probe_cols, first, 0, 1, 32, u, half)
    take_windows(ext, extent, tiles, probe_rows, probe_cols, second, 1, 6, 24, u, half)
    first_cos, first_sin = transmission(first, 0)
    second_cos, second_sin = transmission(second, REACH)
    wave = probe_function(table[...], u, half)
    result = propagate(wave, first_cos, first_sin, second_cos, second_sin, table.shape[0])
    out[0:32, :] = result[:, 0:8]
    out[32:64, :] = result[:, 64:72]


def body(atom_counts, beam_index, beam_weight, probe_rows, probe_cols):
    slices, strip, cols = atom_counts.shape
    count = lax.axis_size("tile")
    forward = [(i, (i + 1) % count) for i in range(count)]
    backward = [(j, i) for i, j in forward]
    prev = lax.ppermute(atom_counts[:, strip - HALO :], "tile", forward)
    following = lax.ppermute(atom_counts[:, :HALO], "tile", backward)
    row = jnp.concatenate([beam_index.astype(F32), beam_weight[:, None]], axis=1)
    table = lax.all_gather(jnp.pad(row, ((0, 0), (0, 125))), "beam", axis=0, tiled=True)
    smem = pl.BlockSpec(memory_space=pltpu.SMEM)
    vmem = pl.BlockSpec(memory_space=pltpu.VMEM)
    return pl.pallas_call(
        kernel,
        out_shape=jax.ShapeDtypeStruct((probe_rows.shape[0], 8), F32),
        in_specs=[smem, smem, vmem, vmem, vmem, vmem],
        out_specs=vmem,
        scratch_shapes=[
            pltpu.VMEM((slices * (strip + 2 * HALO) * cols // 128, 128), F32),
            pltpu.VMEM((32 * 32, 128), F32),
            pltpu.VMEM((24 * 32, 128), F32),
        ],
        compiler_params=pltpu.CompilerParams(vmem_limit_bytes=40 * 2**20),
    )(probe_rows, probe_cols, atom_counts, prev, following, table)


def solution(mesh):
    return jax.shard_map(
        body,
        mesh=mesh,
        in_specs=(P(None, "tile", None), P("beam", None), P("beam"), P("tile"), P("tile")),
        out_specs=P("tile", "beam"),
        check_vma=False,
    )
```

time: 385 us -> 144 us (0.37)
  the two profiles are of different devices: /device:TPU:25 before, /device:TPU:0 now
where the time goes in v1:
time: 144 us
  blocking collectives  119 us (83%)
  starting transfers between devices  16.4 us (11%)
  Pallas kernels  5.66 us (4%)
  local copies, waits for them, and re-layouts  2.46 us (2%)
    all_gather x1, blocking collectives, body(): lax.all_gather(jnp.pad(row, ((0, 0), (0, 125))), 'beam', axis=0, tiled=True)  119 us
    ppermute x1, starting transfers between devices, body(): following = lax.ppermute(atom_counts[:, :HALO], 'tile', backward)  14.5 us
    pallas_call x1, Pallas kernels, body(): pl.pallas_call(kernel, out_shape=jax.ShapeDtypeStruct((probe_rows.shape[0...  5.66 us
  transfers between devices with their start and end apart: 2, of which 0 were waited for; matrix products, arithmetic and copies ran while one was open for 0% of the time, Pallas kernels for 0%

profile of v1, /device:TPU:0, one launch (start us, length us, event | category | flops | bytes accessed | tf_op | source)
XLA Modules:
  0.0 144.3 jit_solution(14533826532475406494)
XLA Ops:
  0.0 0.0 copy-start
  0.0 1.1 fusion.2
  1.1 1.9 %collective-permute-start = (bf16[2,16,4096]{2,1,0:T(8,128)(2,1)S(1)}, bf16[2,16,4096]{2,1,0:T(8,128)(2,1)S(1)}, u32[]{:S(2)}, u32[]{:S(2)}) collective-permute-start(bf16[2,16,4096]{2,1,0:T(8,128)(2,1)S(1)} %get-tuple-element.6), channel_id=1, source_target_pairs={{0,1},{1,2},{2,3},{3,4},{4,5},{5,6},{6,7},{7,8},{8,9},{9,10},{10,1... | collective-permute-start | bytes 786440 | tf_op jit(solution)/shard_map/ppermute | solution.py:240
  3.1 0.0 copy-start.3
  3.1 14.5 %collective-permute-start.1 = (bf16[2,16,4096]{2,1,0:T(8,128)(2,1)S(1)}, bf16[2,16,4096]{2,1,0:T(8,128)(2,1)S(1)}, u32[]{:S(2)}, u32[]{:S(2)}) collective-permute-start(bf16[2,16,4096]{2,1,0:T(8,128)(2,1)S(1)} %get-tuple-element.5), channel_id=1, source_target_pairs={{1,0},{2,1},{3,2},{4,3},{5,4},{6,5},{7,6},{8,7},{9,8},{10,9},{11,1... | collective-permute-start | bytes 786440 | tf_op jit(solution)/shard_map/ppermute | solution.py:241
  18.2 0.0 copy-done.3
  18.2 0.1 fusion.1
  18.3 119.0 %all-gather = f32[32,1,128]{2,1,0:T(1,128)S(1)} all-gather(f32[1,1,128]{2,1,0:T(1,128)S(1)} %fusion.1), channel_id=1, replica_groups=mesh['beam'=32,'tile'=16] {'beam'}, dimensions={0}, use_global_device_ids=true | all-gather | bytes 16896 | tf_op jit(solution)/shard_map/all_gather | solution.py:243
  137.3 0.0 copy-start.1
  137.3 0.0 copy-start.2
  137.3 0.0 collective-permute-done.prev
  137.3 0.0 collective-permute-done.1.following
  137.3 0.0 copy-done
  137.3 0.6 copy-done.1
  137.9 0.0 copy-done.2
  138.0 5.7 %shard_map.55 = f32[64,8]{1,0:T(8,128)S(1)} custom-call(s32[64]{0:T(128)S(1)} %copy-done.1, s32[64]{0:T(128)S(1)} %copy-done.2, bf16[2,32,4096]{2,1,0:T(8,128)(2,1)S(1)} %copy-done, bf16[2,16,4096]{2,1,0:T(8,128)(2,1)S(1)} %collective-permute-done.prev, bf16[2,16,4096]{2,1,0:T(8,128)(2,1)S(1)} %collective-permute-done.1.following, f32[32,128]{1,0:T(8,128)S(1)} %bitcast.5), custom_call_target="tpu_custom_call" | custom-call | tf_op jit(solution)/shard_map/pallas_call | solution.py:246
  143.6 0.7 copy.8
  (1 shorter events, 0.0 us)
Async XLA Ops:
  0.0 137.3 %copy-start = (bf16[2,32,4096]{2,1,0:T(8,128)(2,1)S(1)}, bf16[2,32,4096]{2,1,0:T(8,128)(2,1)}, u32[]{:S(2)}) copy-start(bf16[2,32,4096]{2,1,0:T(8,128)(2,1)} %own.1) | copy-start | bytes 1572868
  1.1 136.2 %collective-permute-start = (bf16[2,16,4096]{2,1,0:T(8,128)(2,1)S(1)}, bf16[2,16,4096]{2,1,0:T(8,128)(2,1)S(1)}, u32[]{:S(2)}, u32[]{:S(2)}) collective-permute-start(bf16[2,16,4096]{2,1,0:T(8,128)(2,1)S(1)} %get-tuple-element.6), channel_id=1, source_target_pairs={{0,1},{1,2},{2,3},{3,4},{4,5},{5,6},{6,7},{7,8},{8,9},{9,10},{10,1... | collective-permute-start | bytes 786440 | tf_op jit(solution)/shard_map/ppermute | solution.py:240
  3.1 15.1 %copy-start.3 = (s32[1,2]{1,0:T(1,128)S(1)}, s32[1,2]{1,0:T(1,128)}, u32[]{:S(2)}) copy-start(s32[1,2]{1,0:T(1,128)} %param.6) | copy-start | bytes 28
  3.1 134.2 %collective-permute-start.1 = (bf16[2,16,4096]{2,1,0:T(8,128)(2,1)S(1)}, bf16[2,16,4096]{2,1,0:T(8,128)(2,1)S(1)}, u32[]{:S(2)}, u32[]{:S(2)}) collective-permute-start(bf16[2,16,4096]{2,1,0:T(8,128)(2,1)S(1)} %get-tuple-element.5), channel_id=1, source_target_pairs={{1,0},{2,1},{3,2},{4,3},{5,4},{6,5},{7,6},{8,7},{9,8},{10,9},{11,1... | collective-permute-start | bytes 786440 | tf_op jit(solution)/shard_map/ppermute | solution.py:241
  137.3 0.7 copy-start.1
  137.3 0.7 copy-start.2

commit v2 on v1

--- a/solution.py
+++ b/solution.py
@@ -15,6 +15,7 @@
 CENTRE = 1.2
 F32 = jnp.float32
 BF16 = jnp.bfloat16
+MESH = pl.DeviceIdType.MESH
 
 
 def make_taps():
@@ -136,6 +137,19 @@
             block = source[s, :, pl.ds(pl.multiple_of(tile * 128, 128), 128)]
             start = pl.multiple_of((s * tiles + tile) * extent + first, 16)
             ext[pl.ds(start, rows), :] = block.astype(F32)
+        return carry
+
+    lax.fori_loop(0, tiles, one, 0, unroll=4)
+
+
+def place_halo(ext, halo, s, extent, strip):
+    tiles = halo.shape[3] // 128
+
+    def one(tile, carry):
+        for side, first in ((0, 0), (1, HALO + strip)):
+            block = halo[side, s, :, pl.ds(pl.multiple_of(tile * 128, 128), 128)]
+            start = pl.multiple_of((s * tiles + tile) * extent + first, 16)
+            ext[pl.ds(start, HALO), :] = block.astype(F32)
         return carry
 
     lax.fori_loop(0, tiles, one, 0, unroll=4)
@@ -213,48 +227,250 @@
     return (both[:, :128] * both[:, :128] + both[:, 128:] * both[:, 128:]) * (1.0 / beams)
 
 
-def kernel(probe_rows, probe_cols, own, prev, following, table, out, ext, first, second):
-    beam = lax.axis_index("beam")
+def kernel(
+    probe_rows, probe_cols, beam_index, beam_weight, counts, out,
+    own, halo, table, ext, first, second,
+    own_sem, halo_send, halo_recv, share_send, share_recv, row_send, row_recv,
+    table_send, table_recv, ready,
+):
+    beam, tile = lax.axis_index("beam"), lax.axis_index("tile")
+    tiles_total = lax.axis_size("tile")
+    group = 8
+    lines = lax.axis_size("beam") // group
+    half_tiles = tiles_total // 2
+    x, place = beam // group, lax.rem(beam, group)
+    early = tile < half_tiles
+    across_up = lax.rem(tile, half_tiles) == half_tiles - 1
+    across_down = lax.rem(tile, half_tiles) == 0
+    mirrored = x * group + (group - 1 - place)
+    up = (jnp.where(across_up, mirrored, beam), lax.rem(tile + 1, tiles_total))
+    down = (jnp.where(across_down, mirrored, beam), lax.rem(tile + tiles_total - 1, tiles_total))
+    other_half = (beam, lax.rem(tile + half_tiles, tiles_total))
+    slices, strip, cols = own.shape
+    part = cols // lines
+
+    def member(line, z):
+        return line * group + z
+
+    own_copy = pltpu.make_async_copy(counts, own, own_sem)
+    own_copy.start()
+
+    barrier = pltpu.get_barrier_semaphore()
+
+    def tell(device):
+        pl.semaphore_signal(barrier, inc=1, device_id=device, device_id_type=MESH)
+
+    for step in range(1, lines):
+        tell((member(lax.rem(x + step, lines), place), tile))
+    for device, across in ((up, across_up), (down, across_down)):
+
+        @pl.when(jnp.logical_or(early, jnp.logical_not(across)))
+        def _():
+            tell(device)
+
+    @pl.when(early)
+    def _():
+        tell(other_half)
+
+        def tell_later(z, carry):
+            for line in range(lines):
+                tell((member(line, z), tile))
+            return carry
+
+        lax.fori_loop(place + 1, group, tell_later, 0)
+
+    lane = lax.broadcasted_iota(jnp.int32, (1, 128), 1)
+
+    @pl.when(early)
+    def _():
+        kx = beam_index[0, 0].astype(F32)
+        ky = beam_index[0, 1].astype(F32)
+        table[beam] = jnp.where(
+            lane == 0, kx, jnp.where(lane == 1, ky, jnp.where(lane == 2, beam_weight[0], 0.0))
+        )
+
+    across_any = jnp.logical_or(across_up, across_down).astype(jnp.int32)
+    expected = (lines - 1) + 2 - across_any
+    expected = expected + jnp.where(early, lines * place, 1 + across_any)
+    pl.semaphore_wait(barrier, expected)
+
+    def row_copy(peer):
+        return pltpu.make_async_remote_copy(
+            src_ref=table.at[beam], dst_ref=table.at[beam], send_sem=row_send.at[peer],
+            recv_sem=row_recv.at[beam], device_id=(peer, tile), device_id_type=MESH,
+        )
+
+    def row_arrival(peer):
+        return pltpu.make_async_remote_copy(
+            src_ref=table.at[peer], dst_ref=table.at[peer], send_sem=row_send.at[peer],
+            recv_sem=row_recv.at[peer], device_id=(peer, tile), device_id_type=MESH,
+        )
+
+    table_copy = pltpu.make_async_remote_copy(
+        src_ref=table, dst_ref=table, send_sem=table_send, recv_sem=table_recv,
+        device_id=other_half, device_id_type=MESH,
+    )
+
+    @pl.when(early)
+    def _():
+        for step in range(1, lines):
+            row_copy(member(lax.rem(x + step, lines), place)).start()
+
+        def send_back(z, carry):
+            for line in range(lines):
+                row_copy(member(line, z)).start()
+            return carry
+
+        lax.fori_loop(0, place, send_back, 0)
+
+    @pl.when(jnp.logical_not(early))
+    def _():
+        pl.semaphore_signal(ready, inc=1, device_id=other_half, device_id_type=MESH)
+
+    my_part = pl.ds(pl.multiple_of(x * part, part), part)
+
+    def halo_copy(side, s):
+        rows = pl.ds(strip - HALO, HALO) if side == 0 else pl.ds(0, HALO)
+        return pltpu.make_async_remote_copy(
+            src_ref=own.at[s, rows, my_part], dst_ref=halo.at[side, s, :, my_part],
+            send_sem=halo_send.at[side, s], recv_sem=halo_recv.at[side, s],
+            device_id=up if side == 0 else down, device_id_type=MESH,
+        )
+
+    def share_copy(side, s, step):
+        return pltpu.make_async_remote_copy(
+            src_ref=halo.at[side, s, :, my_part], dst_ref=halo.at[side, s, :, my_part],
+            send_sem=share_send.at[side, s, step - 1], recv_sem=share_recv.at[side, s, step - 1],
+            device_id=(member(lax.rem(x + step, lines), place), tile), device_id_type=MESH,
+        )
+
+    def share_arrival(side, s, step):
+        theirs = lax.rem(x + lines - step, lines)
+        where = pl.ds(pl.multiple_of(theirs * part, part), part)
+        return pltpu.make_async_remote_copy(
+            src_ref=halo.at[side, s, :, where], dst_ref=halo.at[side, s, :, where],
+            send_sem=share_send.at[side, s, step - 1], recv_sem=share_recv.at[side, s, step - 1],
+            device_id=(member(theirs, place), tile), device_id_type=MESH,
+        )
+
+    own_copy.wait()
+    for s in range(slices):
+        for side, across in ((0, across_up), (1, across_down)):
+
+            @pl.when(jnp.logical_not(jnp.logical_and(early, across)))
+            def _():
+                halo_copy(side, s).start()
+
+    extent = strip + 2 * HALO
+    place_rows(ext, own, HALO, extent)
+
+    for s in range(slices):
+        for side, across in ((0, across_down), (1, across_up)):
+            halo_copy(side, s).wait_recv()
+
+            @pl.when(jnp.logical_and(early, across))
+            def _():
+                halo_copy(1 - side, s).start()
+
+            for step in range(1, lines):
+                share_copy(side, s, step).start()
+
+    @pl.when(early)
+    def _():
+        def answer(z, carry):
+            for line in range(lines):
+                peer = member(line, z)
+                row_arrival(peer).wait_recv()
+                row_copy(peer).start()
+            return carry
+
+        lax.fori_loop(place + 1, group, answer, 0)
+        for step in range(1, lines):
+            row_arrival(member(lax.rem(x + step, lines), place)).wait_recv()
+
+        def collect(z, carry):
+            for line in range(lines):
+                row_arrival(member(line, z)).wait_recv()
+            return carry
+
+        lax.fori_loop(0, place, collect, 0)
+        pl.semaphore_wait(ready, 1)
+        table_copy.start()
+
+    @pl.when(jnp.logical_not(early))
+    def _():
+        table_copy.wait_recv()
+
     u, half = beam // 2, lax.rem(beam, 2)
-    strip = own.shape[1]
-    tiles = own.shape[2] // 128
-    extent = strip + 2 * HALO
-    place_rows(ext, prev, 0, extent)
-    place_rows(ext, own, HALO, extent)
-    place_rows(ext, following, HALO + strip, extent)
-    take_windows(ext, extent, tiles, probe_rows, probe_cols, first, 0, 1, 32, u, half)
-    take_windows(ext, extent, tiles, probe_rows, probe_cols, second, 1, 6, 24, u, half)
-    first_cos, first_sin = transmission(first, 0)
-    second_cos, second_sin = transmission(second, REACH)
-    wave = probe_function(table[...], u, half)
-    result = propagate(wave, first_cos, first_sin, second_cos, second_sin, table.shape[0])
-    out[0:32, :] = result[:, 0:8]
-    out[32:64, :] = result[:, 64:72]
+    tiles = cols // 128
+    wave = probe_function(table[:, 0, :], u, half)
+
+    parts = []
+    for s, (gathered, row, count, shift) in enumerate(
+        ((first, 1, 32, 0), (second, 6, 24, REACH))
+    ):
+        for side in (0, 1):
+            for step in range(1, lines):
+                share_arrival(side, s, step).wait_recv()
+        place_halo(ext, halo, s, extent, strip)
+        take_windows(ext, extent, tiles, probe_rows, probe_cols, gathered, s, row, count, u, half)
+        parts.extend(transmission(gathered, shift))
+    result = propagate(wave, *parts, table.shape[0])
+    turned = jnp.transpose(result)
+    out[:, 0:32] = turned[0:8]
+    out[:, 32:64] = turned[64:72]
+
+    for s in range(slices):
+        for side in (0, 1):
+            halo_copy(side, s).wait_send()
+            for step in range(1, lines):
+                share_copy(side, s, step).wait_send()
+
+    @pl.when(early)
+    def _():
+        table_copy.wait_send()
+
+        def sent(step, carry):
+            row_copy(lax.rem(beam + step, lines * group)).wait_send()
+            return carry
+
+        lax.fori_loop(1, lines * group, sent, 0)
 
 
 def body(atom_counts, beam_index, beam_weight, probe_rows, probe_cols):
     slices, strip, cols = atom_counts.shape
-    count = lax.axis_size("tile")
-    forward = [(i, (i + 1) % count) for i in range(count)]
-    backward = [(j, i) for i, j in forward]
-    prev = lax.ppermute(atom_counts[:, strip - HALO :], "tile", forward)
-    following = lax.ppermute(atom_counts[:, :HALO], "tile", backward)
-    row = jnp.concatenate([beam_index.astype(F32), beam_weight[:, None]], axis=1)
-    table = lax.all_gather(jnp.pad(row, ((0, 0), (0, 125))), "beam", axis=0, tiled=True)
+    beams = lax.axis_size("beam")
+    lines = beams // 8
     smem = pl.BlockSpec(memory_space=pltpu.SMEM)
-    vmem = pl.BlockSpec(memory_space=pltpu.VMEM)
-    return pl.pallas_call(
+    dma = pltpu.SemaphoreType.DMA
+    result = pl.pallas_call(
         kernel,
-        out_shape=jax.ShapeDtypeStruct((probe_rows.shape[0], 8), F32),
-        in_specs=[smem, smem, vmem, vmem, vmem, vmem],
-        out_specs=vmem,
+        out_shape=jax.ShapeDtypeStruct((8, probe_rows.shape[0]), F32),
+        in_specs=[smem, smem, smem, smem, pl.BlockSpec(memory_space=pltpu.HBM)],
+        out_specs=pl.BlockSpec(memory_space=pltpu.VMEM),
         scratch_shapes=[
+            pltpu.VMEM((slices, strip, cols), BF16),
+            pltpu.VMEM((2, slices, HALO, cols), BF16),
+            pltpu.VMEM((beams, 1, 128), F32),
             pltpu.VMEM((slices * (strip + 2 * HALO) * cols // 128, 128), F32),
             pltpu.VMEM((32 * 32, 128), F32),
             pltpu.VMEM((24 * 32, 128), F32),
+            dma(()),
+            dma((2, slices)),
+            dma((2, slices)),
+            dma((2, slices, lines - 1)),
+            dma((2, slices, lines - 1)),
+            dma((beams,)),
+            dma((beams,)),
+            dma(()),
+            dma(()),
+            pltpu.SemaphoreType.REGULAR,
         ],
-        compiler_params=pltpu.CompilerParams(vmem_limit_bytes=40 * 2**20),
-    )(probe_rows, probe_cols, atom_counts, prev, following, table)
+        compiler_params=pltpu.CompilerParams(
+            collective_id=0, has_side_effects=True, vmem_limit_bytes=40 * 2**20
+        ),
+    )(probe_rows, probe_cols, beam_index, beam_weight, atom_counts)
+    return result.T
 
 
 def solution(mesh):

time: 144 us -> 36.6 us (0.25)
  the two profiles are of different devices: /device:TPU:0 before, /device:TPU:480 now
where the time goes in v2:
time: 36.6 us; the launch traced here: 36.4 us
  Pallas kernels  34.1 us (93%)
  local copies, waits for them, and re-layouts  1.64 us (4%)
  between operations  0.74 us (2%)
    pallas_call x1, Pallas kernels, body(): pl.pallas_call(kernel, out_shape=jax.ShapeDtypeStruct((8, probe_rows.shap...  34.1 us
    unnamed x9, local copies, waits for them, and re-layouts  1.64 us

profile of v2, /device:TPU:480, one launch (start us, length us, event | category | flops | bytes accessed | tf_op | source)
XLA Modules:
  0.0 36.4 jit_solution(15393934925158867836)
XLA Ops:
  0.0 0.0 copy-start.2
  0.0 0.0 copy-start.1
  0.0 0.0 copy-start.3
  0.7 0.0 copy-done.2
  0.7 0.0 copy-done.1
  0.7 0.0 copy-done.3
  0.7 0.0 copy-start
  0.7 1.0 %copy-done = bf16[2,32,4096]{2,1,0:T(8,128)(2,1)S(1)} copy-done((bf16[2,32,4096]{2,1,0:T(8,128)(2,1)S(1)}, bf16[2,32,4096]{2,1,0:T(8,128)(2,1)}, u32[]{:S(2)}) %copy-start) | copy-done | bytes 524312
  1.8 34.1 %shard_map.55 = f32[8,64]{1,0:T(8,128)S(1)} custom-call(s32[64]{0:T(128)S(1)} %copy-done.1, s32[64]{0:T(128)S(1)} %copy-done.2, s32[1,2]{1,0:T(1,128)S(1)} %copy-done.3, f32[1]{0:T(128)S(6)} %copy.7.beam_weight, bf16[2,32,4096]{2,1,0:T(8,128)(2,1)S(1)} %copy-done), custom_call_target="tpu_custom_call" | custom-call | tf_op jit(solution)/shard_map/pallas_call | solution.py:446
  35.8 0.6 %copy.8 = f32[64,8]{0,1:T(8,128)} copy(f32[64,8]{0,1:T(8,128)S(1)} %bitcast.1) | data formatting | bytes 4096
Async XLA Ops:
  0.0 0.7 %copy-start.2 = (s32[64]{0:T(128)S(1)}, s32[64]{0:T(128)}, u32[]{:S(2)}) copy-start(s32[64]{0:T(128)} %probe_cols.1) | copy-start | bytes 772
  0.0 0.7 %copy-start.1 = (s32[64]{0:T(128)S(1)}, s32[64]{0:T(128)}, u32[]{:S(2)}) copy-start(s32[64]{0:T(128)} %probe_rows.1) | copy-start | bytes 772
  0.0 0.7 %copy-start.3 = (s32[1,2]{1,0:T(1,128)S(1)}, s32[1,2]{1,0:T(1,128)}, u32[]{:S(2)}) copy-start(s32[1,2]{1,0:T(1,128)} %beam_index.1) | copy-start | bytes 28
  0.7 1.0 %copy-start = (bf16[2,32,4096]{2,1,0:T(8,128)(2,1)S(1)}, bf16[2,32,4096]{2,1,0:T(8,128)(2,1)}, u32[]{:S(2)}) copy-start(bf16[2,32,4096]{2,1,0:T(8,128)(2,1)} %counts.1) | copy-start | bytes 1572868

commit v3 on v2

v3 whole, which is shorter than its diff:
```python
import functools
import math

import jax
import jax.numpy as jnp
import numpy as np
from jax import lax
from jax.experimental import pallas as pl
from jax.experimental.pallas import tpu as pltpu
from jax.sharding import PartitionSpec as P

CROP = 16
REACH = 5
HALO = 16
CENTRE = 1.2
F32 = jnp.float32
BF16 = jnp.bfloat16
MESH = pl.DeviceIdType.MESH


def make_taps():
    offsets = np.arange(-REACH, REACH + 1, dtype=np.float64)
    blur = np.exp(-(offsets**2) / 4.5)
    blur = blur / blur.sum()
    weight = np.exp(-(offsets**2) / 18.0)
    weight = weight / weight.sum()
    spread = weight * np.exp(1j * 0.35 * offsets**2)
    return blur, spread


def fit(function, limit, terms):
    nodes = 0.5 * limit * (1.0 + np.cos(np.pi * (np.arange(64) + 0.5) / 64))
    return np.polynomial.Polynomial.fit(nodes, function(nodes), terms - 1, domain=[0, limit]).convert().coef


def horner(coefs, x):
    result = jnp.full_like(x, float(coefs[-1]))
    for coef in coefs[-2::-1]:
        result = result * x + float(coef)
    return result


def cos_sin_small(t):
    square = t * t
    root = np.sqrt
    even = fit(lambda s: np.cos(root(s)), 1.69, 6)
    odd = fit(lambda s: np.sin(root(s)) / root(s), 1.69, 5)
    return horner(even, square), t * horner(odd, square)


def cos_sin_turns(turns):
    turns = turns - jnp.floor(turns + 0.5)
    square = turns * turns
    full = lambda s: 2.0 * np.pi * np.sqrt(s)
    even = fit(lambda s: np.cos(full(s)), 0.25, 9)
    odd = fit(lambda s: np.sin(full(s)) / np.sqrt(s), 0.25, 8)
    return horner(even, square), turns * horner(odd, square)


def band(distance, values):
    result = jnp.zeros(distance.shape, F32)
    reach = jnp.abs(distance)
    for k in range(REACH + 1):
        result = jnp.where(reach == k, float(values[REACH + k]), result)
    return result


def split(x):
    high = x.astype(BF16)
    return high, (x - high.astype(F32)).astype(BF16)


def blur_matrix(shift):
    blur, _ = make_taps()
    rows = lax.broadcasted_iota(jnp.int32, (128, 128), 0)
    cols = lax.broadcasted_iota(jnp.int32, (128, 128), 1)
    values = band(rows - cols - shift - REACH, 0.6 * blur)
    high, low = split(jnp.where(rows // 64 == cols // 64, values, 0.0))
    return jnp.concatenate([high, low], axis=1)


def spread_matrix():
    _, spread = make_taps()
    turned = spread * np.exp(1j * CENTRE)
    rows = lax.broadcasted_iota(jnp.int32, (128, 128), 0)
    cols = lax.broadcasted_iota(jnp.int32, (128, 128), 1)
    same = rows // 64 == cols // 64
    distance = rows - cols - REACH
    real = jnp.where(same, band(distance, turned.real), 0.0)
    imag = jnp.where(same, band(distance, turned.imag), 0.0)
    whole = jnp.concatenate(
        [jnp.concatenate([real, imag], axis=1), jnp.concatenate([-imag, real], axis=1)], axis=0
    )
    return split(whole)


def dot(a, b):
    return jnp.dot(a, b, preferred_element_type=F32)


def dot3(x, high, low):
    x_high, x_low = split(x)
    return dot(x_high, high) + dot(x_low, high) + dot(x_high, low)


def place_rows(ext, source, first, extent):
    slices, rows, cols = source.shape
    tiles = cols // 128

    def one(tile, carry):
        for s in range(slices):
            block = source[s, :, pl.ds(pl.multiple_of(tile * 128, 128), 128)]
            start = pl.multiple_of((s * tiles + tile) * extent + first, 16)
            ext[pl.ds(start, rows), :] = block.astype(F32)
        return carry

    lax.fori_loop(0, tiles, one, 0, unroll=8)


def place_halo(ext, halo, s, extent, strip):
    tiles = halo.shape[3] // 128

    def one(tile, carry):
        for side, first in ((0, 0), (1, HALO + strip)):
            block = halo[side, s, :, pl.ds(pl.multiple_of(tile * 128, 128), 128)]
            start = pl.multiple_of((s * tiles + tile) * extent + first, 16)
            ext[pl.ds(start, HALO), :] = block.astype(F32)
        return carry

    lax.fori_loop(0, tiles, one, 0, unroll=8)


def take_windows(ext, extent, tiles, rows, cols, gathered, slice_index, first, count, u, half):
    cols_total = tiles * 128
    pairs = rows.shape[0] // 2
    lane = lax.broadcasted_iota(jnp.int32, (count, 128), 1)

    def window(probe, place):
        start = lax.rem(cols[probe] + (8 * half - 3 * REACH + cols_total), cols_total)
        tile, offset = start >> 7, start & 127
        after = lax.rem(tile + 1, tiles)
        row = rows[probe] + (u + first)
        near = ext[pl.ds((slice_index * tiles + tile) * extent + row, count), :]
        far = ext[pl.ds((slice_index * tiles + after) * extent + row, count), :]
        both = jnp.where(lane >= offset, near, far)
        return pltpu.roll(both, (128 - offset + place) & 127, 1)

    def one(pair, carry):
        joined = jnp.where(lane < 64, window(pair, 0), window(pair + pairs, 64))
        gathered[pl.ds(pair, count, stride=pairs), :] = joined
        return carry

    lax.fori_loop(0, pairs, one, 0, unroll=16)


def row_at(i, k):
    return pl.ds(pl.multiple_of((i + k) * 32, 32), 32)


def transmission(gathered, blurred, matrix, trans):
    blur, _ = make_taps()
    both = dot(gathered[...].astype(BF16), matrix[...])
    blurred[0 : gathered.shape[0], :] = both[:, :128] + both[:, 128:]

    def one(i, carry):
        total = float(blur[REACH]) * blurred[row_at(i, REACH), :] - CENTRE
        for k in range(REACH):
            near, far = blurred[row_at(i, k), :], blurred[row_at(i, 2 * REACH - k), :]
            total = total + float(blur[k]) * (near + far)
        trans[0, row_at(i, 0), :], trans[1, row_at(i, 0), :] = cos_sin_small(total)
        return carry

    rows = trans.shape[1] // 32
    lax.fori_loop(0, rows, one, 0, unroll=rows)


def spread_rows(psi, i):
    _, spread = make_taps()
    out_real, out_imag = None, None
    for k in range(REACH + 1):
        a, b = psi[0, row_at(i, k), :], psi[1, row_at(i, k), :]
        if k != REACH:
            a = a + psi[0, row_at(i, 2 * REACH - k), :]
            b = b + psi[1, row_at(i, 2 * REACH - k), :]
        c, s = float(spread[k].real), float(spread[k].imag)
        real, imag = c * a - s * b, c * b + s * a
        out_real = real if out_real is None else out_real + real
        out_imag = imag if out_imag is None else out_imag + imag
    return out_real, out_imag


def probe_function(table, u, half):
    kx, ky, weight = table[:, 0:1], table[:, 1:2], table[:, 2:3]
    lane = lax.broadcasted_iota(jnp.int32, (table.shape[0], 128), 1)
    down = (lane + (u - 2 * REACH)).astype(F32)
    across = (lax.rem(lane, 64) + (8 * half - 2 * REACH)).astype(F32)
    row_cos, row_sin = cos_sin_turns(kx * down * (1.0 / 512.0))
    col_cos, col_sin = cos_sin_turns(ky * across * (1.0 / 4096.0))
    left = jnp.concatenate([weight * row_cos, weight * row_sin], axis=0)
    right = jnp.concatenate(
        [
            jnp.concatenate([col_cos, col_sin], axis=1),
            jnp.concatenate([-col_sin, col_cos], axis=1),
        ],
        axis=0,
    )
    return lax.dot_general(
        left, right, (((0,), (0,)), ((), ())), precision=lax.Precision.HIGHEST,
        preferred_element_type=F32,
    )


def propagate(wave_ref, trans0, trans1, psi, both, spread, beams):
    rows0, rows1 = trans0.shape[1] // 32, trans1.shape[1] // 32

    def enter(i, carry):
        cos, sin = trans0[0, row_at(i, 0), :], trans0[1, row_at(i, 0), :]
        real = wave_ref[pl.ds(i, 1), 0:128]
        imag = wave_ref[pl.ds(i, 1), 128:256]
        psi[0, row_at(i, 0), :] = cos * real - sin * imag
        psi[1, row_at(i, 0), :] = cos * imag + sin * real
        return carry

    lax.fori_loop(0, rows0, enter, 0, unroll=rows0)

    def between(i, carry):
        both[row_at(i, 0), 0:128], both[row_at(i, 0), 128:256] = spread_rows(psi, i)
        return carry

    lax.fori_loop(0, rows1, between, 0, unroll=rows1)
    both[...] = dot3(both[...], spread[0], spread[1])

    def again(i, carry):
        real, imag = both[row_at(i, 0), 0:128], both[row_at(i, 0), 128:256]
        cos, sin = trans1[0, row_at(i, 0), :], trans1[1, row_at(i, 0), :]
        psi[0, row_at(i, 0), :] = real * cos - imag * sin
        psi[1, row_at(i, 0), :] = real * sin + imag * cos
        return carry

    lax.fori_loop(0, rows1, again, 0, unroll=rows1)
    last = dot3(jnp.concatenate(spread_rows(psi, 0), axis=1), spread[0], spread[1])
    return (last[:, :128] * last[:, :128] + last[:, 128:] * last[:, 128:]) * (1.0 / beams)


def kernel(
    rows_hbm, cols_hbm, index_hbm, weight_hbm, counts, out,
    probe_rows, probe_cols, beam_index, beam_weight,
    own, halo, table, ext, first, second, blurred, matrix0, matrix1, spread,
    trans0, trans1, wave, psi, both,
    own_sem, small_sem, halo_send, halo_recv, share_send, share_recv, row_send, row_recv,
    table_send, table_recv, ready, hello, ready_edge,
):
    beam, tile = lax.axis_index("beam"), lax.axis_index("tile")
    tiles_total = lax.axis_size("tile")
    group = 8
    lines = lax.axis_size("beam") // group
    half_tiles = tiles_total // 2
    x, place = beam // group, lax.rem(beam, group)
    early = tile < half_tiles
    late = jnp.logical_not(early)
    across_up = lax.rem(tile, half_tiles) == half_tiles - 1
    across_down = lax.rem(tile, half_tiles) == 0
    across = jnp.logical_or(across_up, across_down)
    mirrored = x * group + (group - 1 - place)
    up = (jnp.where(across_up, mirrored, beam), lax.rem(tile + 1, tiles_total))
    down = (jnp.where(across_down, mirrored, beam), lax.rem(tile + tiles_total - 1, tiles_total))
    other_half = (mirrored, lax.rem(tile + half_tiles, tiles_total))
    slices, strip, cols = own.shape
    part = cols // lines
    on_first = tile == 0
    first_one = jnp.logical_and(on_first, beam == 0)
    skip_first = on_first.astype(jnp.int32)
    skip_line = jnp.logical_and(on_first, place == 0).astype(jnp.int32)

    def member(line, z):
        return line * group + z

    def slot(line, z):
        return z * lines + line

    def line_peer(step):
        return member(lax.rem(x + step, lines), place)

    my_part = pl.ds(pl.multiple_of(x * part, part), part)
    edge_rows = (pl.ds(strip - HALO, HALO), pl.ds(0, HALO))
    own_copies = [
        pltpu.make_async_copy(
            counts.at[s, edge_rows[side]], own.at[s, edge_rows[side]], own_sem.at[side, s]
        )
        for s in range(slices)
        for side in (0, 1)
    ]
    for copy in own_copies:
        copy.start()
    small_copies = [
        pltpu.make_async_copy(source, target, small_sem.at[k])
        for k, (source, target) in enumerate(
            (
                (index_hbm, beam_index), (weight_hbm, beam_weight),
                (rows_hbm, probe_rows), (cols_hbm, probe_cols),
            )
        )
    ]
    for copy in small_copies:
        copy.start()

    barrier = pltpu.get_barrier_semaphore()

    def tell(device):
        pl.semaphore_signal(barrier, inc=1, device_id=device, device_id_type=MESH)

    @pl.when(jnp.logical_and(on_first, beam > 0))
    def _():
        tell((0, 0))

    for device, far in ((up, across_up), (down, across_down)):

        @pl.when(jnp.logical_or(early, jnp.logical_not(far)))
        def _():
            tell(device)

    def tell_line(line, carry):
        tell((member(line, place), tile))
        return carry

    def tell_later(z, carry):
        for line in range(lines):
            tell((member(line, z), tile))
        return carry

    @pl.when(jnp.logical_not(first_one))
    def _():
        lax.fori_loop(x + 1, lines, tell_line, 0)

    @pl.when(early)
    def _():
        tell(other_half)

        @pl.when(jnp.logical_not(first_one))
        def _():
            lax.fori_loop(place + 1, group, tell_later, 0)


    lane = lax.broadcasted_iota(jnp.int32, (1, 128), 1)
    small_copies[0].wait()
    small_copies[1].wait()

    @pl.when(early)
    def _():
        kx = beam_index[0, 0].astype(F32)
        ky = beam_index[0, 1].astype(F32)
        table[slot(x, place)] = jnp.where(
            lane == 0, kx, jnp.where(lane == 1, ky, jnp.where(lane == 2, beam_weight[0], 0.0))
        )

    across_count = across.astype(jnp.int32)
    expected = x + jnp.where(early, lines * place, 1 + across_count) - skip_first
    expected = jnp.where(first_one, lines * group - 1, expected) + 2 - across_count
    pl.semaphore_wait(barrier, expected)

    my_slot = slot(x, place)

    def row_copy(line, z):
        return pltpu.make_async_remote_copy(
            src_ref=table.at[my_slot], dst_ref=table.at[my_slot], send_sem=row_send,
            recv_sem=row_recv.at[my_slot], device_id=(member(line, z), tile), device_id_type=MESH,
        )

    def row_arrival(line, z):
        theirs = slot(line, z)
        return pltpu.make_async_remote_copy(
            src_ref=table.at[theirs], dst_ref=table.at[theirs], send_sem=row_send,
            recv_sem=row_recv.at[theirs], device_id=(member(line, z), tile), device_id_type=MESH,
        )

    table_copy = pltpu.make_async_remote_copy(
        src_ref=table, dst_ref=table, send_sem=table_send, recv_sem=table_recv,
        device_id=other_half, device_id_type=MESH,
    )

    def send_line(line, carry):
        row_copy(line, place).start()
        return carry

    def send_all(z, carry):
        for line in range(lines):
            row_copy(line, z).start()
        return carry

    @pl.when(jnp.logical_and(early, place > 0))
    def _():
        @pl.when(jnp.logical_not(on_first))
        def _():
            row_copy(0, 0).start()

        for line in range(1, lines):
            row_copy(line, 0).start()
        lax.fori_loop(1, place, send_all, 0)

    @pl.when(early)
    def _():
        lax.fori_loop(skip_line, x, send_line, 0)

    @pl.when(first_one)
    def _():
        lax.fori_loop(1, lines, send_line, 0)
        lax.fori_loop(1, group, send_all, 0)

    @pl.when(late)
    def _():
        pl.semaphore_signal(ready, inc=1, device_id=other_half, device_id_type=MESH)
        for device, far in ((up, across_up), (down, across_down)):

            @pl.when(far)
            def _():
                pl.semaphore_signal(ready_edge, inc=1, device_id=device, device_id_type=MESH)

    def hello_line(line, carry):
        pl.semaphore_signal(
            hello, inc=1, device_id=(member(line, place), tile), device_id_type=MESH
        )
        return carry

    lax.fori_loop(skip_line, x, hello_line, 0)

    def halo_copy(side, s, far):
        where = my_part if far else pl.ds(0, cols)
        return pltpu.make_async_remote_copy(
            src_ref=own.at[s, edge_rows[side], where], dst_ref=halo.at[side, s, :, where],
            send_sem=halo_send.at[side, s], recv_sem=halo_recv.at[side, s],
            device_id=up if side == 0 else down, device_id_type=MESH,
        )

    def share_copy(side, s, step):
        return pltpu.make_async_remote_copy(
            src_ref=halo.at[side, s, :, my_part], dst_ref=halo.at[side, s, :, my_part],
            send_sem=share_send, recv_sem=share_recv.at[side, s, step - 1],
            device_id=(line_peer(step), tile), device_id_type=MESH,
        )

    def share_arrival(side, s, step):
        theirs = lax.rem(x + lines - step, lines)
        where = pl.ds(pl.multiple_of(theirs * part, part), part)
        return pltpu.make_async_remote_copy(
            src_ref=halo.at[side, s, :, where], dst_ref=halo.at[side, s, :, where],
            send_sem=share_send, recv_sem=share_recv.at[side, s, step - 1],
            device_id=(member(theirs, place), tile), device_id_type=MESH,
        )

    for copy in own_copies:
        copy.wait()
    for s in range(slices):
        for side, far in ((0, across_up), (1, across_down)):

            @pl.when(jnp.logical_and(late, far))
            def _():
                halo_copy(side, s, True).start()

            @pl.when(jnp.logical_not(far))
            def _():
                halo_copy(side, s, False).start()

    small_copies[2].wait()
    small_copies[3].wait()
    u, half = beam // 2, lax.rem(beam, 2)
    tiles = cols // 128
    extent = strip + 2 * HALO
    matrix0[...] = blur_matrix(0)
    matrix1[...] = blur_matrix(REACH)
    spread[0], spread[1] = spread_matrix()
    place_rows(ext, own, HALO, extent)

    @pl.when(jnp.logical_and(x < lines - 1, jnp.logical_not(first_one)))
    def _():
        pl.semaphore_wait(hello, lines - 1 - x)

    @pl.when(jnp.logical_and(early, jnp.logical_not(first_one)))
    def _():
        lax.fori_loop(x + 1, lines, send_line, 0)

    def collect(z, carry):
        for line in range(lines):
            row_arrival(line, z).wait_recv()
        return carry

    def answer(z, carry):
        for line in range(lines):
            row_arrival(line, z).wait_recv()
            row_copy(line, z).start()
        return carry

    answer_first = jnp.logical_or(across, place >= group // 2)

    @pl.when(jnp.logical_and(jnp.logical_and(early, answer_first), jnp.logical_not(first_one)))
    def _():
        lax.fori_loop(place + 1, group, answer, 0)

    for side, far in ((0, across_up), (1, across_down)):

        @pl.when(jnp.logical_and(early, far))
        def _():
            pl.semaphore_wait(ready_edge, 1)
            for s in range(slices):
                halo_copy(side, s, True).start()

    def collect_rows():
        @pl.when(jnp.logical_not(answer_first))
        def _():
            lax.fori_loop(place + 1, group, answer, 0)

        @pl.when(jnp.logical_and(on_first, place > 0))
        def _():
            row_arrival(0, 0).wait_recv()
            row_copy(0, 0).start()

        def collect_line(line, carry):
            row_arrival(line, place).wait_recv()
            return carry

        def collect_head(line, carry):
            row_arrival(line, 0).wait_recv()
            return carry

        lax.fori_loop(skip_line, x, collect_line, 0)
        lax.fori_loop(x + 1, lines, collect_line, 0)

        @pl.when(place > 0)
        def _():
            lax.fori_loop(skip_first, lines, collect_head, 0)

        lax.fori_loop(1, place, collect, 0)

        @pl.when(first_one)
        def _():
            lax.fori_loop(1, group, collect, 0)

        pl.semaphore_wait(ready, 1)
        table_copy.start()

    beside_first = jnp.logical_and(skip_line == 1, beam > 0)

    @pl.when(beside_first)
    def _():
        row_arrival(0, 0).wait_recv()
        row_copy(0, 0).start()

    for s in range(slices):
        for side, far in ((0, across_down), (1, across_up)):

            @pl.when(far)
            def _():
                halo_copy(side, s, True).wait_recv()
                for step in range(1, lines):
                    share_copy(side, s, step).start()


    @pl.when(jnp.logical_and(jnp.logical_and(early, across), jnp.logical_not(first_one)))
    def _():
        collect_rows()

    for s, (gathered, row, count, matrix, trans) in enumerate(
        ((first, 1, 32, matrix0, trans0), (second, 6, 24, matrix1, trans1))
    ):
        for side, far in ((0, across_down), (1, across_up)):

            @pl.when(far)
            def _():
                for step in range(1, lines):
                    share_arrival(side, s, step).wait_recv()

            @pl.when(jnp.logical_not(far))
            def _():
                halo_copy(side, s, False).wait_recv()

        place_halo(ext, halo, s, extent, strip)
        take_windows(ext, extent, tiles, probe_rows, probe_cols, gathered, s, row, count, u, half)
        transmission(gathered, blurred, matrix, trans)

    @pl.when(jnp.logical_or(first_one, jnp.logical_and(early, jnp.logical_not(across))))
    def _():
        collect_rows()

    @pl.when(late)
    def _():
        table_copy.wait_recv()

    wave[...] = probe_function(table[:, 0, :], u, half)
    result = propagate(wave, trans0, trans1, psi, both, spread, table.shape[0])
    turned = jnp.transpose(result)
    out[:, 0:32] = turned[0:8]
    out[:, 32:64] = turned[64:72]

    def sent(ref, semaphore):
        pltpu.make_async_remote_copy(
            src_ref=ref, dst_ref=ref, send_sem=semaphore, recv_sem=table_recv,
            device_id=other_half, device_id_type=MESH,
        ).wait_send()

    for s in range(slices):
        for side, far in ((0, across_up), (1, across_down)):

            @pl.when(far)
            def _():
                halo_copy(side, s, True).wait_send()

            @pl.when(jnp.logical_not(far))
            def _():
                halo_copy(side, s, False).wait_send()

    @pl.when(across)
    def _():
        sent(halo.at[0, :, :, pl.ds(0, (lines - 1) * part)], share_send)


    @pl.when(early)
    def _():
        table_copy.wait_send()

        sent(table.at[pl.ds(0, lines * group - 1)], row_send)


def body(atom_counts, beam_index, beam_weight, probe_rows, probe_cols):
    slices, strip, cols = atom_counts.shape
    beams = lax.axis_size("beam")
    lines = beams // 8
    hbm = pl.BlockSpec(memory_space=pltpu.HBM)
    dma = pltpu.SemaphoreType.DMA
    result = pl.pallas_call(
        kernel,
        out_shape=jax.ShapeDtypeStruct((8, probe_rows.shape[0]), F32),
        in_specs=[hbm] * 5,
        out_specs=pl.BlockSpec(memory_space=pltpu.VMEM),
        scratch_shapes=[
            pltpu.SMEM(probe_rows.shape, jnp.int32),
            pltpu.SMEM(probe_cols.shape, jnp.int32),
            pltpu.SMEM(beam_index.shape, jnp.int32),
            pltpu.SMEM(beam_weight.shape, F32),
            pltpu.VMEM((slices, strip, cols), BF16),
            pltpu.VMEM((2, slices, HALO, cols), BF16),
            pltpu.VMEM((beams, 1, 128), F32),
            pltpu.VMEM((slices * (strip + 2 * HALO) * cols // 128, 128), F32),
            pltpu.VMEM((32 * 32, 128), F32),
            pltpu.VMEM((24 * 32, 128), F32),
            pltpu.VMEM((32 * 32, 128), F32),
            pltpu.VMEM((128, 256), BF16),
            pltpu.VMEM((128, 256), BF16),
            pltpu.VMEM((2, 256, 256), BF16),
            pltpu.VMEM((2, 21 * 32, 128), F32),
            pltpu.VMEM((2, 11 * 32, 128), F32),
            pltpu.VMEM((128, 256), F32),
            pltpu.VMEM((2, 21 * 32, 128), F32),
            pltpu.VMEM((11 * 32, 256), F32),
            dma((2, slices)),
            dma((4,)),
            dma((2, slices)),
            dma((2, slices)),
            dma(()),
            dma((2, slices, lines - 1)),
            dma(()),
            dma((beams,)),
            dma(()),
            dma(()),
            pltpu.SemaphoreType.REGULAR,
            pltpu.SemaphoreType.REGULAR,
            pltpu.SemaphoreType.REGULAR,
        ],
        compiler_params=pltpu.CompilerParams(
            collective_id=0, has_side_effects=True, vmem_limit_bytes=64 * 2**20 - 2**18
        ),
    )(probe_rows, probe_cols, beam_index, beam_weight, atom_counts)
    return result.T


def solution(mesh):
    return jax.shard_map(
        body,
        mesh=mesh,
        in_specs=(P(None, "tile", None), P("beam", None), P("beam"), P("tile"), P("tile")),
        out_specs=P("tile", "beam"),
        check_vma=False,
    )
```

time: 36.6 us -> 29.3 us (0.80)
  Pallas kernels: 34.1 us -> 27.2 us
    pallas_call x1, Pallas kernels: 34.1 us -> 27.2 us  [body(): pl.pallas_call(kernel, out_shape=jax.ShapeDtypeStruct((8, probe_rows.shap...]
    unnamed x9 -> x1, local copies, waits for them, and re-layouts: 1.64 us -> 1.28 us
where the time goes in v3:
time: 29.3 us; the launch traced here: 29.2 us
  Pallas kernels  27.2 us (93%)
  local copies, waits for them, and re-layouts  1.28 us (4%)
  between operations  0.66 us (2%)
    pallas_call x1, Pallas kernels, body(): pl.pallas_call(kernel, out_shape=jax.ShapeDtypeStruct((8, probe_rows.shap...  27.2 us
    unnamed x1, local copies, waits for them, and re-layouts  1.28 us

profile of v3, /device:TPU:480, one launch (start us, length us, event | category | flops | bytes accessed | tf_op | source)
XLA Modules:
  0.0 29.2 jit_solution(17115304252842638329)
XLA Ops:
  0.7 27.2 %shard_map.55 = f32[8,64]{1,0:T(8,128)} custom-call(s32[64]{0:T(128)} %rows_hbm.1, s32[64]{0:T(128)} %cols_hbm.1, s32[1,2]{1,0:T(1,128)} %index_hbm.1, f32[1]{0:T(128)S(6)} %copy.7.weight_hbm, bf16[2,32,4096]{2,1,0:T(8,128)(2,1)} %counts.1), custom_call_target="tpu_custom_call" | custom-call | tf_op jit(solution)/shard_map/pallas_call | solution.py:628
  27.9 1.3 %copy.8 = f32[64,8]{0,1:T(8,128)} copy(f32[64,8]{0,1:T(8,128)} %bitcast.1) | data formatting | bytes 4096

commit v4 on v3

--- a/solution.py
+++ b/solution.py
@@ -627,7 +627,7 @@
     dma = pltpu.SemaphoreType.DMA
     result = pl.pallas_call(
         kernel,
-        out_shape=jax.ShapeDtypeStruct((8, probe_rows.shape[0]), F32),
+        out_shape=pltpu.VMEM((8, probe_rows.shape[0]), F32),
         in_specs=[hbm] * 5,
         out_specs=pl.BlockSpec(memory_space=pltpu.VMEM),
         scratch_shapes=[

time: 29.3 us -> 28 us (0.956)
  local copies, waits for them, and re-layouts: 1.28 us -> 0.6 us
  Pallas kernels: 27.2 us -> 26.6 us
    unnamed x1, local copies, waits for them, and re-layouts: 1.28 us -> 0.6 us
    pallas_call x1, Pallas kernels: 27.2 us -> 26.6 us  [body(): pl.pallas_call(kernel, out_shape=pltpu.VMEM((8, probe_rows.shape[0]), F32...]
where the time goes in v4:
time: 28 us; the launch traced here: 27.9 us
  Pallas kernels  26.6 us (95%)
  between operations  0.66 us (2%)
  local copies, waits for them, and re-layouts  0.6 us (2%)
    pallas_call x1, Pallas kernels, body(): pl.pallas_call(kernel, out_shape=pltpu.VMEM((8, probe_rows.shape[0]), F32...  26.6 us
    unnamed x1, local copies, waits for them, and re-layouts  0.6 us

profile of v4, /device:TPU:480, one launch (start us, length us, event | category | flops | bytes accessed | tf_op | source)
XLA Modules:
  0.0 27.9 jit_solution(14316153033581931800)
XLA Ops:
  0.7 26.6 %shard_map.55 = f32[8,64]{1,0:T(8,128)S(1)} custom-call(s32[64]{0:T(128)} %rows_hbm.1, s32[64]{0:T(128)} %cols_hbm.1, s32[1,2]{1,0:T(1,128)} %index_hbm.1, f32[1]{0:T(128)S(6)} %copy.8.weight_hbm, bf16[2,32,4096]{2,1,0:T(8,128)(2,1)} %counts.1), custom_call_target="tpu_custom_call" | custom-call | tf_op jit(solution)/shard_map/pallas_call | solution.py:628
  27.3 0.6 %copy.7 = f32[64,8]{0,1:T(8,128)} copy(f32[64,8]{0,1:T(8,128)S(1)} %bitcast.1) | data formatting | bytes 4096

commit v5 on v4

--- a/solution.py
+++ b/solution.py
@@ -245,10 +245,10 @@
 def kernel(
     rows_hbm, cols_hbm, index_hbm, weight_hbm, counts, out,
     probe_rows, probe_cols, beam_index, beam_weight,
-    own, halo, table, ext, first, second, blurred, matrix0, matrix1, spread,
+    own, halo, table, whole, ext, first, second, blurred, matrix0, matrix1, spread,
     trans0, trans1, wave, psi, both,
     own_sem, small_sem, halo_send, halo_recv, share_send, share_recv, row_send, row_recv,
-    table_send, table_recv, ready, hello, ready_edge,
+    table_send, table_recv, first_send, first_recv, ready, hello, ready_edge,
 ):
     beam, tile = lax.axis_index("beam"), lax.axis_index("tile")
     tiles_total = lax.axis_size("tile")
@@ -304,6 +304,8 @@
     for copy in small_copies:
         copy.start()
 
+    whole[...] = jnp.zeros(whole.shape, F32)
+
     barrier = pltpu.get_barrier_semaphore()
 
     def tell(device):
@@ -373,6 +375,15 @@
             recv_sem=row_recv.at[theirs], device_id=(member(line, z), tile), device_id_type=MESH,
         )
 
+    feeder = jnp.logical_and(on_first, beam == group)
+    first_copy = pltpu.make_async_remote_copy(
+        src_ref=table, dst_ref=whole, send_sem=first_send, recv_sem=first_recv,
+        device_id=(0, 0), device_id_type=MESH,
+    )
+    first_table_copy = pltpu.make_async_remote_copy(
+        src_ref=whole, dst_ref=table, send_sem=table_send, recv_sem=table_recv,
+        device_id=other_half, device_id_type=MESH,
+    )
     table_copy = pltpu.make_async_remote_copy(
         src_ref=table, dst_ref=table, send_sem=table_send, recv_sem=table_recv,
         device_id=other_half, device_id_type=MESH,
@@ -489,12 +500,6 @@
             row_copy(line, z).start()
         return carry
 
-    answer_first = jnp.logical_or(across, place >= group // 2)
-
-    @pl.when(jnp.logical_and(jnp.logical_and(early, answer_first), jnp.logical_not(first_one)))
-    def _():
-        lax.fori_loop(place + 1, group, answer, 0)
-
     for side, far in ((0, across_up), (1, across_down)):
 
         @pl.when(jnp.logical_and(early, far))
@@ -503,6 +508,12 @@
             for s in range(slices):
                 halo_copy(side, s, True).start()
 
+    answer_first = jnp.logical_or(across, place >= group // 2)
+
+    @pl.when(jnp.logical_and(jnp.logical_and(early, answer_first), jnp.logical_not(first_one)))
+    def _():
+        lax.fori_loop(place + 1, group, answer, 0)
+
     def collect_rows():
         @pl.when(jnp.logical_not(answer_first))
         def _():
@@ -511,7 +522,6 @@
         @pl.when(jnp.logical_and(on_first, place > 0))
         def _():
             row_arrival(0, 0).wait_recv()
-            row_copy(0, 0).start()
 
         def collect_line(line, carry):
             row_arrival(line, place).wait_recv()
@@ -522,7 +532,10 @@
             return carry
 
         lax.fori_loop(skip_line, x, collect_line, 0)
-        lax.fori_loop(x + 1, lines, collect_line, 0)
+
+        @pl.when(jnp.logical_not(first_one))
+        def _():
+            lax.fori_loop(x + 1, lines, collect_line, 0)
 
         @pl.when(place > 0)
         def _():
@@ -532,17 +545,28 @@
 
         @pl.when(first_one)
         def _():
-            lax.fori_loop(1, group, collect, 0)
+            first_copy.wait_recv()
+
+        @pl.when(feeder)
+        def _():
+            first_copy.start()
 
         pl.semaphore_wait(ready, 1)
-        table_copy.start()
+
+        @pl.when(first_one)
+        def _():
+            first_table_copy.start()
+
+        @pl.when(jnp.logical_not(first_one))
+        def _():
+            table_copy.start()
+
 
     beside_first = jnp.logical_and(skip_line == 1, beam > 0)
 
     @pl.when(beside_first)
     def _():
         row_arrival(0, 0).wait_recv()
-        row_copy(0, 0).start()
 
     for s in range(slices):
         for side, far in ((0, across_down), (1, across_up)):
@@ -584,7 +608,8 @@
     def _():
         table_copy.wait_recv()
 
-    wave[...] = probe_function(table[:, 0, :], u, half)
+    rows = jnp.where(first_one, whole[:, 0, :], table[:, 0, :])
+    wave[...] = probe_function(rows, u, half)
     result = propagate(wave, trans0, trans1, psi, both, spread, table.shape[0])
     turned = jnp.transpose(result)
     out[:, 0:32] = turned[0:8]
@@ -616,7 +641,18 @@
     def _():
         table_copy.wait_send()
 
-        sent(table.at[pl.ds(0, lines * group - 1)], row_send)
+
+        @pl.when(jnp.logical_and(on_first, beam > 0))
+        def _():
+            sent(table.at[pl.ds(0, lines * group - 2)], row_send)
+
+        @pl.when(jnp.logical_not(jnp.logical_and(on_first, beam > 0)))
+        def _():
+            sent(table.at[pl.ds(0, lines * group - 1)], row_send)
+
+    @pl.when(feeder)
+    def _():
+        first_copy.wait_send()
 
 
 def body(atom_counts, beam_index, beam_weight, probe_rows, probe_cols):
@@ -637,6 +673,7 @@
             pltpu.SMEM(beam_weight.shape, F32),
             pltpu.VMEM((slices, strip, cols), BF16),
             pltpu.VMEM((2, slices, HALO, cols), BF16),
+            pltpu.VMEM((beams, 1, 128), F32),
             pltpu.VMEM((beams, 1, 128), F32),
             pltpu.VMEM((slices * (strip + 2 * HALO) * cols // 128, 128), F32),
             pltpu.VMEM((32 * 32, 128), F32),
@@ -660,6 +697,8 @@
             dma((beams,)),
             dma(()),
             dma(()),
+            dma(()),
+            dma(()),
             pltpu.SemaphoreType.REGULAR,
             pltpu.SemaphoreType.REGULAR,
             pltpu.SemaphoreType.REGULAR,

time: 28 us -> 27.2 us (0.971)
  the two profiles are of different devices: /device:TPU:480 before, /device:TPU:96 now
where the time goes in v5:
time: 27.2 us; the launch traced here: 27 us
  Pallas kernels  25.8 us (95%)
  between operations  0.66 us (2%)
  local copies, waits for them, and re-layouts  0.6 us (2%)
    pallas_call x1, Pallas kernels, body(): pl.pallas_call(kernel, out_shape=pltpu.VMEM((8, probe_rows.shape[0]), F32...  25.8 us
    unnamed x1, local copies, waits for them, and re-layouts  0.6 us

profile of v5, /device:TPU:96, one launch (start us, length us, event | category | flops | bytes accessed | tf_op | source)
XLA Modules:
  0.0 27.0 jit_solution(14252940818163311466)
XLA Ops:
  0.7 25.8 %shard_map.55 = f32[8,64]{1,0:T(8,128)S(1)} custom-call(s32[64]{0:T(128)} %rows_hbm.1, s32[64]{0:T(128)} %cols_hbm.1, s32[1,2]{1,0:T(1,128)} %index_hbm.1, f32[1]{0:T(128)S(6)} %copy.8.weight_hbm, bf16[2,32,4096]{2,1,0:T(8,128)(2,1)} %counts.1), custom_call_target="tpu_custom_call" | custom-call | tf_op jit(solution)/shard_map/pallas_call | solution.py:664
  26.4 0.6 %copy.7 = f32[64,8]{0,1:T(8,128)} copy(f32[64,8]{0,1:T(8,128)S(1)} %bitcast.1) | data formatting | bytes 4096

commit v6 on v5

--- a/solution.py
+++ b/solution.py
@@ -117,20 +117,30 @@
     lax.fori_loop(0, tiles, one, 0, unroll=8)
 
 
-def place_halo(ext, halo, s, extent, strip):
+def place_halo(ext, halo, side, s, extent, strip):
     tiles = halo.shape[3] // 128
 
     def one(tile, carry):
-        for side, first in ((0, 0), (1, HALO + strip)):
-            block = halo[side, s, :, pl.ds(pl.multiple_of(tile * 128, 128), 128)]
-            start = pl.multiple_of((s * tiles + tile) * extent + first, 16)
-            ext[pl.ds(start, HALO), :] = block.astype(F32)
+        block = halo[side, s, :, pl.ds(pl.multiple_of(tile * 128, 128), 128)]
+        start = pl.multiple_of((s * tiles + tile) * extent + side * (HALO + strip), 16)
+        ext[pl.ds(start, HALO), :] = block.astype(F32)
         return carry
 
     lax.fori_loop(0, tiles, one, 0, unroll=8)
 
 
-def take_windows(ext, extent, tiles, rows, cols, gathered, slice_index, first, count, u, half):
+def clear_halo(ext, side, s, tiles, extent, strip):
+    def one(tile, carry):
+        start = pl.multiple_of((s * tiles + tile) * extent + side * (HALO + strip), 16)
+        ext[pl.ds(start, HALO), :] = jnp.zeros((HALO, 128), F32)
+        return carry
+
+    lax.fori_loop(0, tiles, one, 0, unroll=8)
+
+
+def take_windows(
+    ext, extent, tiles, rows, cols, gathered, slice_index, first, count, u, half, base=0
+):
     cols_total = tiles * 128
     pairs = rows.shape[0] // 2
     lane = lax.broadcasted_iota(jnp.int32, (count, 128), 1)
@@ -139,7 +149,7 @@
         start = lax.rem(cols[probe] + (8 * half - 3 * REACH + cols_total), cols_total)
         tile, offset = start >> 7, start & 127
         after = lax.rem(tile + 1, tiles)
-        row = rows[probe] + (u + first)
+        row = rows[probe] + (u + first + base)
         near = ext[pl.ds((slice_index * tiles + tile) * extent + row, count), :]
         far = ext[pl.ds((slice_index * tiles + after) * extent + row, count), :]
         both = jnp.where(lane >= offset, near, far)
@@ -147,10 +157,10 @@
 
     def one(pair, carry):
         joined = jnp.where(lane < 64, window(pair, 0), window(pair + pairs, 64))
-        gathered[pl.ds(pair, count, stride=pairs), :] = joined
-        return carry
-
-    lax.fori_loop(0, pairs, one, 0, unroll=16)
+        gathered[pl.ds(base * pairs + pair, count, stride=pairs), :] = joined
+        return carry
+
+    lax.fori_loop(0, pairs, one, 0, unroll=8)
 
 
 def row_at(i, k):
@@ -494,6 +504,32 @@
             row_arrival(line, z).wait_recv()
         return carry
 
+    windows = ((first, 1, 32, matrix0, trans0), (second, 6, 24, matrix1, trans1))
+
+    def near_windows():
+        for s, (gathered, row, count, _, _) in enumerate(windows):
+            for side, far in ((0, across_down), (1, across_up)):
+
+                @pl.when(jnp.logical_not(far))
+                def _():
+                    halo_copy(side, s, False).wait_recv()
+                    place_halo(ext, halo, side, s, extent, strip)
+
+            take_windows(
+                ext, extent, tiles, probe_rows, probe_cols, gathered, s, row, count, u, half
+            )
+
+    @pl.when(across)
+    def _():
+        for s in range(slices):
+            for side, far in ((0, across_down), (1, across_up)):
+
+                @pl.when(far)
+                def _():
+                    clear_halo(ext, side, s, tiles, extent, strip)
+
+        near_windows()
+
     def answer(z, carry):
         for line in range(lines):
             row_arrival(line, z).wait_recv()
@@ -582,22 +618,24 @@
     def _():
         collect_rows()
 
-    for s, (gathered, row, count, matrix, trans) in enumerate(
-        ((first, 1, 32, matrix0, trans0), (second, 6, 24, matrix1, trans1))
-    ):
+    for s, (gathered, row, _, matrix, trans) in enumerate(windows):
+        if s == 0:
+            @pl.when(jnp.logical_not(across))
+            def _():
+                near_windows()
+
         for side, far in ((0, across_down), (1, across_up)):
 
             @pl.when(far)
             def _():
                 for step in range(1, lines):
                     share_arrival(side, s, step).wait_recv()
-
-            @pl.when(jnp.logical_not(far))
-            def _():
-                halo_copy(side, s, False).wait_recv()
-
-        place_halo(ext, halo, s, extent, strip)
-        take_windows(ext, extent, tiles, probe_rows, probe_cols, gathered, s, row, count, u, half)
+                place_halo(ext, halo, side, s, extent, strip)
+                take_windows(
+                    ext, extent, tiles, probe_rows, probe_cols, gathered, s, row, 16, u, half,
+                    base=0 if side == 0 else gathered.shape[0] // 32 - 16,
+                )
+
         transmission(gathered, blurred, matrix, trans)
 
     @pl.when(jnp.logical_or(first_one, jnp.logical_and(early, jnp.logical_not(across))))

time: 27.2 us -> 27.2 us (level)
  no operation moved by 1% of the time
where the time goes in v6:
time: 27.2 us; the launch traced here: 27.1 us
  Pallas kernels  25.8 us (95%)
  between operations  0.66 us (2%)
  local copies, waits for them, and re-layouts  0.6 us (2%)
    pallas_call x1, Pallas kernels, body(): pl.pallas_call(kernel, out_shape=pltpu.VMEM((8, probe_rows.shape[0]), F32...  25.8 us
    unnamed x1, local copies, waits for them, and re-layouts  0.6 us

profile of v6, /device:TPU:96, one launch (start us, length us, event | category | flops | bytes accessed | tf_op | source)
XLA Modules:
  0.0 27.1 jit_solution(5797663271517737403)
XLA Ops:
  0.7 25.8 %shard_map.55 = f32[8,64]{1,0:T(8,128)S(1)} custom-call(s32[64]{0:T(128)} %rows_hbm.1, s32[64]{0:T(128)} %cols_hbm.1, s32[1,2]{1,0:T(1,128)} %index_hbm.1, f32[1]{0:T(128)S(6)} %copy.8.weight_hbm, bf16[2,32,4096]{2,1,0:T(8,128)(2,1)} %counts.1), custom_call_target="tpu_custom_call" | custom-call | tf_op jit(solution)/shard_map/pallas_call | solution.py:702
  26.5 0.6 %copy.7 = f32[64,8]{0,1:T(8,128)} copy(f32[64,8]{0,1:T(8,128)S(1)} %bitcast.1) | data formatting | bytes 4096
